TPU v7x, 128 devices: a whole 4x4x4 slice. The times are simulated.
128 devices in a mesh: dp: 8 (over x, y_hi), feat: 16 (over y_lo, z, core).
Axes of the slice: x: 4, y: 4 (y_hi: 2, y_lo: 2; y = y_hi * 2 + y_lo), z: 4, core: 2. Of those that a mesh axis runs over, the one named last changes fastest.
Arguments:
- tokens: bfloat16 [8192, 128, 128], P('dp', 'feat'), may hold values from -6 to 6
- cotangent: bfloat16 [8192, 128, 128], P('dp', 'feat'), may hold values from -6 to 6
- left_up_factor: bfloat16 [128, 128, 128], P('feat', 'dp'), may hold values from -0.5 to 0.5
- right_up_factor: bfloat16 [128, 128, 512], P('feat', 'dp'), may hold values from -0.5 to 0.5
- left_out: bfloat16 [128, 512, 128], P('feat', 'dp'), may hold values from -0.25 to 0.25
- right_out: bfloat16 [128, 128, 128], P('feat', 'dp'), may hold values from -0.5 to 0.5
Outputs:
- output: bfloat16 [8192, 128, 128], P('dp', 'feat')
- token_input_gradient: bfloat16 [8192, 128, 128], P('dp', 'feat')
- grad_left_in: float32 [128, 128, 128], P('feat', 'dp')
- grad_right_in: float32 [128, 128, 512], P('feat', 'dp')
- grad_left_out: float32 [128, 512, 128], P('feat', 'dp')
- grad_right_out: float32 [128, 128, 128], P('feat', 'dp')
All inputs are finite; a program needn't handle non-finite values.
Results may differ from a plain program's by a relative error of at most 0.0068.
Values may be sent and summed in bfloat16 or wider, within the bound.
A program may use at most 128 MiB of HBM per device.

v0:
```python
import jax
import jax.numpy as jnp
from jax import lax
from jax.sharding import PartitionSpec as P


def phi_cdf(value):
    return 0.5 * (1.0 + jax.scipy.special.erf(value * 0.7071067811865476))


def gelu_slope(value):
    return phi_cdf(value) + value * jnp.exp(-0.5 * value * value) * 0.3989422804014327


def factor_product(form, first, second):
    return jnp.einsum(form, first, second, preferred_element_type=jnp.float32)


def on_device(tokens, cotangent, left_up_factor, right_up_factor, left_out, right_out):
    total_rows = tokens.shape[0] * lax.axis_size("dp")
    init_scale = jnp.float32(1.0) / jnp.sqrt(jnp.float32(total_rows))
    left_up_complete, right_up_complete, full_l2, full_r2 = (
        lax.all_gather(left_up_factor, "dp", axis=1, tiled=True),
        lax.all_gather(right_up_factor, "dp", axis=1, tiled=True),
        lax.all_gather(left_out, "dp", axis=1, tiled=True),
        lax.all_gather(right_out, "dp", axis=1, tiled=True),
    )
    mixed_hidden = factor_product("oqj,qjy->oqy", tokens, left_up_complete).astype(jnp.bfloat16)
    spread_tokens = lax.all_to_all(mixed_hidden, "feat", split_axis=2, concat_axis=1, tiled=True)
    preactivation = factor_product("vub,buo->vbo", spread_tokens, right_up_complete)
    active = (preactivation * phi_cdf(preactivation)).astype(jnp.bfloat16)
    folded = factor_product("tce,cef->tcf", active, full_l2).astype(jnp.bfloat16)
    gathered_fold = lax.all_to_all(folded, "feat", split_axis=2, concat_axis=1, tiled=True)
    output = factor_product("tcf,fcj->tfj", gathered_fold, full_r2).astype(jnp.bfloat16)
    grad_r2 = factor_product("tcf,tfj->fcj", gathered_fold, cotangent) * init_scale
    back_folded = factor_product("tfj,fcj->tcf", cotangent, full_r2).astype(jnp.bfloat16)
    back_local = lax.all_to_all(back_folded, "feat", split_axis=1, concat_axis=2, tiled=True)
    grad_l2 = factor_product("tce,tcf->cef", active, back_local) * init_scale
    preactivation_gradient = (
        factor_product("tcf,cef->tce", back_local, full_l2) * gelu_slope(preactivation)
    ).astype(jnp.bfloat16)
    right_up_gradient = (
        factor_product("owk,okq->kwq", spread_tokens, preactivation_gradient) * init_scale
    )
    spread_gradient = factor_product(
        "qyp,ydp->qdy", preactivation_gradient, right_up_complete
    ).astype(jnp.bfloat16)
    mixed_gradient = lax.all_to_all(
        spread_gradient, "feat", split_axis=1, concat_axis=2, tiled=True
    )
    left_up_gradient = factor_product("hlz,hlr->lzr", tokens, mixed_gradient) * init_scale
    token_input_gradient = factor_product("yfv,fsv->yfs", mixed_gradient, left_up_complete).astype(
        jnp.bfloat16
    )
    share_l1, share_r1, share_l2, share_r2 = (
        lax.psum_scatter(left_up_gradient, "dp", scatter_dimension=1, tiled=True),
        lax.psum_scatter(right_up_gradient, "dp", scatter_dimension=1, tiled=True),
        lax.psum_scatter(grad_l2, "dp", scatter_dimension=1, tiled=True),
        lax.psum_scatter(grad_r2, "dp", scatter_dimension=1, tiled=True),
    )
    return (output, token_input_gradient, share_l1, share_r1, share_l2, share_r2)


def solution(mesh):
    placed = (
        P("dp", "feat", None),
        P("dp", "feat", None),
        P("feat", "dp", None),
        P("feat", "dp", None),
        P("feat", "dp", None),
        P("feat", "dp", None),
    )
    return jax.shard_map(
        on_device,
        mesh=mesh,
        in_specs=placed,
        out_specs=(
            P("dp", "feat", None),
            P("dp", "feat", None),
            P("feat", "dp", None),
            P("feat", "dp", None),
            P("feat", "dp", None),
            P("feat", "dp", None),
        ),
        check_vma=False,
    )
```

profile of v0, /device:TPU:96, one launch (start us, length us, event | category | flops | bytes accessed | tf_op | source)
XLA Modules:
  0.0 543.5 jit_solution(3927192153534008932)
XLA Ops:
  7.2 34.8 %all_gather.12 = bf16[8,128,128]{2,1,0:T(8,128)(2,1)S(1)} all-gather(bf16[8,16,128]{2,1,0:T(8,128)(2,1)} %param.8), channel_id=1, replica_groups=mesh['dp'=8,'feat'=16] {'dp'}, dimensions={1}, use_global_device_ids=true | all-gather | bytes 294912 | tf_op jit(solution)/shard_map/all_gather | solution.py:23
  45.3 5.7 %all-to-all-start = ((bf16[1024,8,128]{0,1,2:T(8,128)(2,1)}), bf16[1024,8,128]{0,1,2:T(8,128)(2,1)}, u32[]{:S(2)}, u32[]{:S(2)}) async-start(bf16[1024,8,128]{0,1,2:T(8,128)(2,1)} %copy.72), calls=%async_computation | async-start | bytes 4194304 | tf_op jit(solution)/shard_map/all_to_all | solution.py:29
  51.7 56.3 %all_gather.15 = bf16[8,128,128]{2,1,0:T(8,128)(2,1)S(1)} all-gather(bf16[8,16,128]{2,1,0:T(8,128)(2,1)S(1)} %copy-done.5), channel_id=1, replica_groups=mesh['dp'=8,'feat'=16] {'dp'}, dimensions={1}, use_global_device_ids=true | all-gather | bytes 294912 | tf_op jit(solution)/shard_map/all_gather | solution.py:26
  112.7 6.8 %all-to-all-start.2 = ((bf16[1024,128,8]{0,2,1:T(8,128)(2,1)}), bf16[1024,128,8]{0,2,1:T(8,128)(2,1)}, u32[]{:S(2)}, u32[]{:S(2)}) async-start(bf16[1024,128,8]{0,2,1:T(8,128)(2,1)} %copy.81), calls=%async_computation.2 | async-start | bytes 4194304 | tf_op jit(solution)/shard_map/all_to_all | solution.py:37
  120.2 4.3 copy.74
  124.6 10.9 %fusion.9 = (bf16[1024,8,512]{2,0,1:T(8,128)(2,1)}, f32[8,1024,512]{2,1,0:T(8,128)}) fusion(bf16[8,128,512]{2,1,0:T(8,128)(2,1)} %all-gather.3.cloned.1.call-done, bf16[1024,128,8]{0,2,1:T(8,128)(2,1)} %bitcast.76), kind=kOutput, calls=%fused_computation.12 | convolution fusion | flops 1094713344 | bytes 28311552 | tf_op jit(solution)/shard_map/vub,buo->vbo/dot_general | solution.py:16
  135.5 32.9 %all-gather.5.cloned.1.call-done = bf16[8,512,128]{2,1,0:T(8,128)(2,1)} async-done(((bf16[8,64,128]{2,1,0:T(8,128)(2,1)}), bf16[8,512,128]{2,1,0:T(8,128)(2,1)}) %all-gather.5.cloned.1.call-update) | async-done | bytes 1048592 | tf_op jit(solution)/shard_map/all_gather | solution.py:25
  168.4 11.1 %fusion.5 = bf16[1024,8,512]{2,0,1:T(8,128)(2,1)S(1)} fusion(f32[8,1024,512]{2,1,0:T(8,128)} %get-tuple-element.31, bf16[8,512,128]{2,1,0:T(8,128)(2,1)} %all-gather.5.cloned.1.call-done, bf16[1024,8,16,8]{0,3,1,2:T(8,128)(2,1)} %bitcast.14), kind=kOutput, calls=%fused_computation.6 | convolution fusion | flops 1115684864 | bytes 28311552 | tf_op jit(solution)/shard_map/tcf,cef->tce/dot_general | solution.py:16
  182.8 3.7 convert_bitcast_fusion.1
  186.4 4.2 copy.84
  190.6 4.8 all-to-all-start.3
  195.3 7.3 %convert_bitcast_fusion.4 = bf16[1024,8,128]{2,0,1:T(8,128)(2,1)} fusion(bf16[1024,8,512]{2,0,1:T(8,128)(2,1)} %get-tuple-element.30, bf16[8,512,128]{2,1,0:T(8,128)(2,1)} %all-gather.5.cloned.1.call-done), kind=kOutput, calls=%fused_computation.24 | convolution fusion | flops 1074790400 | bytes 11534336 | tf_op jit(solution)/shard_map/tce,cef->tcf/dot_general | solution.py:16
  202.6 4.2 copy.76
  206.8 18.1 %all-to-all-done.3 = bf16[1024,128,8]{0,2,1:T(8,128)(2,1)} async-done(((bf16[1024,128,8]{0,2,1:T(8,128)(2,1)}), bf16[1024,128,8]{0,2,1:T(8,128)(2,1)}, u32[]{:S(2)}, u32[]{:S(2)}) %all-to-all-start.3) | async-done | bytes 2097184 | tf_op jit(solution)/shard_map/all_to_all | solution.py:48
  224.8 4.9 all-to-all-start.1
  233.6 26.6 %all-to-all-done.1 = bf16[1024,8,128]{0,1,2:T(8,128)(2,1)} async-done(((bf16[1024,8,128]{0,1,2:T(8,128)(2,1)}), bf16[1024,8,128]{0,1,2:T(8,128)(2,1)}, u32[]{:S(2)}, u32[]{:S(2)}) %all-to-all-start.1) | async-done | bytes 2097184 | tf_op jit(solution)/shard_map/all_to_all | solution.py:33
  264.7 3.6 fusion.40
  268.4 8.2 %fusion.34 = f32[8,128,512]{2,1,0:T(8,128)} fusion(bf16[1024,8,512]{2,0,1:T(8,128)(2,1)} %copy-done.1, bf16[1024,128,8]{0,2,1:T(8,128)(2,1)} %bitcast.77), kind=kOutput, calls=%fused_computation.41 | convolution fusion | flops 1074266112 | bytes 12582912 | tf_op jit(solution)/shard_map/owk,okq->kwq/dot_general | solution.py:16
  276.9 8.0 %fusion.37 = f32[8,512,128]{2,1,0:T(8,128)} fusion(bf16[1024,8,512]{2,0,1:T(8,128)(2,1)} %get-tuple-element.30, bf16[1024,8,16,8]{0,3,1,2:T(8,128)(2,1)} %bitcast.14), kind=kOutput, calls=%fused_computation.42 | convolution fusion | flops 1074266112 | bytes 12582912 | tf_op jit(solution)/shard_map/tce,tcf->cef/dot_general | solution.py:16
  284.9 3.8 convert_bitcast_fusion.3
  296.5 8.1 %reduce-scatter.5.cloned.1.call-done = f32[8,16,128]{2,0,1:T(8,128)} async-done(((f32[8,128,128]{2,0,1:T(8,128)}), f32[8,16,128]{2,0,1:T(8,128)}) %reduce-scatter.5.cloned.1.call-update) | async-done | bytes 65552 | tf_op jit(solution)/shard_map/reduce_scatter | solution.py:56
  306.1 72.8 %reduce-scatter.11.cloned.1.call-done = f32[8,16,128]{2,1,0:T(8,128)} async-done(((f32[8,128,128]{2,1,0:T(8,128)}), f32[8,16,128]{2,1,0:T(8,128)}) %reduce-scatter.11.cloned.1.call-update) | async-done | bytes 65552 | tf_op jit(solution)/shard_map/reduce_scatter | solution.py:59
  379.0 78.6 %reduce-scatter.7.cloned.1.call-done = f32[8,16,512]{2,1,0:T(8,128)} async-done(((f32[8,128,512]{2,1,0:T(8,128)}), f32[8,16,512]{2,1,0:T(8,128)}) %reduce-scatter.7.cloned.1.call-update) | async-done | bytes 262160 | tf_op jit(solution)/shard_map/reduce_scatter | solution.py:57
  457.6 79.1 %reduce-scatter.9.cloned.1.call-done = f32[8,64,128]{2,1,0:T(8,128)} async-done(((f32[8,512,128]{2,1,0:T(8,128)}), f32[8,64,128]{2,1,0:T(8,128)}) %reduce-scatter.9.cloned.1.call-update) | async-done | bytes 262160 | tf_op jit(solution)/shard_map/reduce_scatter | solution.py:58
  (38 shorter events, 30.7 us)
Async XLA Ops:
  7.2 34.9 %copy-start = (bf16[1024,8,128]{2,1,0:T(8,128)(2,1)S(1)}, bf16[1024,8,128]{2,1,0:T(8,128)(2,1)}, u32[]{:S(2)}) copy-start(bf16[1024,8,128]{2,1,0:T(8,128)(2,1)} %param.6) | copy-start | bytes 6291460
  45.2 6.4 %copy-start.5 = (bf16[8,16,128]{2,1,0:T(8,128)(2,1)S(1)}, bf16[8,16,128]{2,1,0:T(8,128)(2,1)}, u32[]{:S(2)}) copy-start(bf16[8,16,128]{2,1,0:T(8,128)(2,1)} %param.11) | copy-start | bytes 98308
  45.3 67.5 %all-to-all-start = ((bf16[1024,8,128]{0,1,2:T(8,128)(2,1)}), bf16[1024,8,128]{0,1,2:T(8,128)(2,1)}, u32[]{:S(2)}, u32[]{:S(2)}) async-start(bf16[1024,8,128]{0,1,2:T(8,128)(2,1)} %copy.72), calls=%async_computation | async-start | bytes 4194304 | tf_op jit(solution)/shard_map/all_to_all | solution.py:29
  50.9 73.6 %all-gather.3.cloned.1.call-start = ((), (), s32[]{:S(2)}) async-start(), calls=%async_computation.8 | async-start | bytes 1179648 | tf_op jit(solution)/shard_map/all_gather | solution.py:24
  112.7 55.6 %all-to-all-start.2 = ((bf16[1024,128,8]{0,2,1:T(8,128)(2,1)}), bf16[1024,128,8]{0,2,1:T(8,128)(2,1)}, u32[]{:S(2)}, u32[]{:S(2)}) async-start(bf16[1024,128,8]{0,2,1:T(8,128)(2,1)} %copy.81), calls=%async_computation.2 | async-start | bytes 4194304 | tf_op jit(solution)/shard_map/all_to_all | solution.py:37
  119.5 48.9 %all-gather.5.cloned.1.call-start = ((), (), s32[]{:S(2)}) async-start(), calls=%async_computation.9 | async-start | bytes 1179648 | tf_op jit(solution)/shard_map/all_gather | solution.py:25
  168.4 14.4 %copy-start.4 = (bf16[8,128,512]{2,1,0:T(8,128)(2,1)S(1)}, bf16[8,128,512]{2,1,0:T(8,128)(2,1)}, u32[]{:S(2)}) copy-start(bf16[8,128,512]{2,1,0:T(8,128)(2,1)} %all-gather.3.cloned.1.call-done) | copy-start | bytes 3145732
  179.5 3.2 copy-start.1
  190.6 34.2 %all-to-all-start.3 = ((bf16[1024,128,8]{0,2,1:T(8,128)(2,1)}), bf16[1024,128,8]{0,2,1:T(8,128)(2,1)}, u32[]{:S(2)}, u32[]{:S(2)}) async-start(bf16[1024,128,8]{0,2,1:T(8,128)(2,1)} %copy.84), calls=%async_computation.3 | async-start | bytes 4194304 | tf_op jit(solution)/shard_map/all_to_all | solution.py:48
  224.8 35.4 %all-to-all-start.1 = ((bf16[1024,8,128]{0,1,2:T(8,128)(2,1)}), bf16[1024,8,128]{0,1,2:T(8,128)(2,1)}, u32[]{:S(2)}, u32[]{:S(2)}) async-start(bf16[1024,8,128]{0,1,2:T(8,128)(2,1)} %copy.76), calls=%async_computation.1 | async-start | bytes 4194304 | tf_op jit(solution)/shard_map/all_to_all | solution.py:33
  229.7 74.9 %reduce-scatter.5.cloned.1.call-start = ((), (), s32[]{:S(2)}) async-start(), calls=%async_computation.10 | async-start | bytes 589824 | tf_op jit(solution)/shard_map/reduce_scatter | solution.py:56
  233.4 145.6 %reduce-scatter.11.cloned.1.call-start = ((), (), s32[]{:S(2)}) async-start(), calls=%async_computation.13 | async-start | bytes 589824 | tf_op jit(solution)/shard_map/reduce_scatter | solution.py:59
  260.2 4.5 copy-start.3
  263.4 1.3 copy-start.2
  268.4 189.2 %reduce-scatter.7.cloned.1.call-start = ((), (), s32[]{:S(2)}) async-start(), calls=%async_computation.11 | async-start | bytes 2359296 | tf_op jit(solution)/shard_map/reduce_scatter | solution.py:57
  276.6 260.0 %reduce-scatter.9.cloned.1.call-start = ((), (), s32[]{:S(2)}) async-start(), calls=%async_computation.12 | async-start | bytes 2359296 | tf_op jit(solution)/shard_map/reduce_scatter | solution.py:58
Sparse Core Ops, SparseCore 0:
  54.1 50.7 all-gather.2
  122.7 45.6 all-gather.4
  234.1 70.4 reduce-scatter.4
  309.1 69.8 reduce-scatter.10
  383.2 74.3 reduce-scatter.6
  462.2 74.3 reduce-scatter.8
where the time goes:
time: 545 us; the launch traced here: 544 us
  waiting for transfers between devices  317 us (58%)
  blocking collectives  91.1 us (17%)
  matrix products  64.7 us (12%)
  local copies, waits for them, and re-layouts  33.2 us (6%)
  starting transfers between devices  23 us (4%)
  between operations  14.2 us (3%)
    reduce_scatter x1, waiting for transfers between devices, on_device(): lax.psum_scatter(grad_l2, 'dp', scatter_dimension=1, tiled=True)  79.1 us
    reduce_scatter x1, waiting for transfers between devices, on_device(): lax.psum_scatter(right_up_gradient, 'dp', scatter_dimension=1, tiled=True)  78.6 us
    reduce_scatter x1, waiting for transfers between devices, on_device(): lax.psum_scatter(grad_r2, 'dp', scatter_dimension=1, tiled=True)  72.8 us
    dot_general x12, matrix products, factor_product(): return jnp.einsum(form, first, second, preferred_element_type=jnp.float32)  64.7 us
    all_gather x1, blocking collectives, on_device(): lax.all_gather(right_out, 'dp', axis=1, tiled=True)  56.3 us
    all_gather x1, blocking collectives, on_device(): lax.all_gather(left_up_factor, 'dp', axis=1, tiled=True)  34.8 us
    all_gather x1, waiting for transfers between devices, on_device(): lax.all_gather(left_out, 'dp', axis=1, tiled=True)  32.9 us
    all_to_all x1, waiting for transfers between devices, on_device(): lax.all_to_all(folded, 'feat', split_axis=2, concat_axis=1, tiled=True)  26.6 us
  transfers between devices with their start and end apart: 10, of which 7 were waited for; matrix products, arithmetic and copies ran while one was open for 13% of the time, Pallas kernels for 0%

commit v1 on v0

v1 whole, which is shorter than its diff:
```python
import functools

import jax
import jax.numpy as jnp
from jax import lax
from jax.experimental import pallas as pl
from jax.experimental.pallas import tpu as pltpu
from jax.sharding import PartitionSpec as P

MESH = pl.DeviceIdType.MESH
BF = jnp.bfloat16
F32 = jnp.float32
NB = 128
EX = 512
T = 1024
TT = 256
NF = 16
NX = 4
QS = 4
NT = (((1,), (1,)), ((), ()))


def dot(a, b):
    return jnp.dot(a, b, preferred_element_type=F32)


def dot_nt(a, b):
    return lax.dot_general(a, b, NT, preferred_element_type=F32)


def gelu_parts(v):
    bell = jnp.exp2(v * v * (-0.7213475204444817)) * 0.3989422804014327
    t = 1.0 / (1.0 + 0.2316419 * jnp.abs(v))
    poly = 1.330274429 * t - 1.821255978
    poly = poly * t + 1.781477937
    poly = poly * t - 0.356563782
    poly = poly * t + 0.319381530
    tail = bell * (poly * t)
    phi = jnp.where(v >= 0, 1.0 - tail, tail)
    return v * phi, phi + v * bell


def layer(tok_h, cot_h, l_h, r_h, lo_h, r2_h,
          out_h, tg_h, gl_o, gr_o, glo_o, gr2_o,
          tok, cot, lg, rg, log_, r2g,
          a1, a3, a2, a4, s1, s3, s2, s4, z1, z3,
          xc, fc, rt, lot, act, bp, zf, zb, stage_o, stage_t,
          gr_s, glo_s, gl_s, gr2_s, gr_r, glo_r, gl_r, gr2_r,
          gr_y, glo_y, gl_y, gr2_y, gr_yr, glo_yr, gl_yr, gr2_yr,
          in_sem, own_sem, out_sem,
          agy_s, agy_r, agx_s, agx_r, aa_s, aa_r, rx_s, rx_r, ry_s, ry_r):
    dp = lax.axis_index("dp")
    me = lax.axis_index("feat")
    x, yh = lax.div(dp, 2), lax.rem(dp, 2)
    partner = (x * 2 + (1 - yh), me)

    def xpeer(i):
        return (lax.rem(x + i, NX) * 2 + yh, me)

    def fpeer(i):
        return lax.rem(me + i, NF)

    ins = [pltpu.make_async_copy(tok_h, tok, in_sem.at[0]), pltpu.make_async_copy(cot_h, cot, in_sem.at[1])]
    for c in ins:
        c.start()
    facs = [(l_h, lg, 16), (r2_h, r2g, 16), (r_h, rg, 16), (lo_h, log_, 64)]
    own = [pltpu.make_async_copy(sh, g.at[:, pl.ds(pl.multiple_of(dp * n, n), n), :], own_sem.at[k])
           for k, (sh, g, n) in enumerate(facs)]
    for c in own:
        c.start()

    barrier = pltpu.get_barrier_semaphore()

    def greet(i, _):
        pl.semaphore_signal(barrier, inc=1, device_id=(dp, fpeer(i)), device_id_type=MESH)
        return 0

    lax.fori_loop(1, NF, greet, 0)
    for i in range(1, NX):
        pl.semaphore_signal(barrier, inc=1, device_id=xpeer(i), device_id_type=MESH)
    pl.semaphore_signal(barrier, inc=1, device_id=partner, device_id_type=MESH)
    pl.semaphore_wait(barrier, NF - 1 + NX - 1 + 1)

    def remote(src, dst, ss, rs, dev):
        return pltpu.make_async_remote_copy(src_ref=src, dst_ref=dst, send_sem=ss, recv_sem=rs,
                                            device_id=dev, device_id_type=MESH)

    def await_bytes(ref, sem):
        pltpu.make_async_copy(ref, ref, sem).wait()

    for k, (sh, g, n) in enumerate(facs):
        mine = g.at[:, pl.ds(pl.multiple_of(dp * n, n), n), :]
        remote(sh, mine, agy_s.at[k], agy_r.at[k], partner).start()
        for i in range(1, NX):
            remote(sh, mine, agx_s.at[k], agx_r.at[k], xpeer(i)).start()

    def forward_shard(k):
        sh, g, n = facs[k]
        theirs = g.at[:, pl.ds(pl.multiple_of(partner[0] * n, n), n), :]
        await_bytes(theirs, agy_r.at[k])
        for i in range(1, NX):
            remote(theirs, theirs, agx_s.at[k], agx_r.at[k], xpeer(i)).start()

    def gathered(k):
        sh, g, n = facs[k]
        own[k].wait()
        await_bytes(g.at[:, pl.ds(0, 6 * n), :], agx_r.at[k])

    forward_shard(0)
    forward_shard(1)

    def spread(z, a, res, t0):
        for h in range(TT // 128):
            z[t0 // 128 + h, pl.ds(a, NB, stride=8), :] = res[:, h * 128:(h + 1) * 128]

    def send_pair(z, abuf, sbuf, kind, q):
        def one(i, _):
            p = fpeer(i)
            rows = pl.ds(pl.multiple_of(p * 16, 16), 16)
            for tt in range(T // 128):
                piece = z[tt, pl.ds(pl.multiple_of(p * 64 + q * 16, 16), 16), :].astype(BF)
                abuf[q, rows, tt * 128:(tt + 1) * 128] = piece
            return 0

        lax.fori_loop(0, NF, one, 0)
        ship(abuf, sbuf, kind, q)

    def ship(abuf, sbuf, kind, q):
        mine = pl.ds(pl.multiple_of(me * 16, 16), 16)

        def go(i, _):
            p = fpeer(i)
            rows = pl.ds(pl.multiple_of(p * 16, 16), 16)
            remote(abuf.at[q, rows, :], sbuf.at[q, mine, :], aa_s.at[kind, q], aa_r.at[kind, q], (dp, p)).start()
            return 0

        lax.fori_loop(1, NF, go, 0)
        sbuf[q, mine, :] = abuf[q, mine, :]

    def arrived(sbuf, kind, q):
        await_bytes(sbuf.at[q, pl.ds(0, 240), :], aa_r.at[kind, q])

    ins[0].wait()
    gathered(0)
    for a in range(8):
        lt = lg[a].astype(F32).T.astype(BF)
        for t0 in range(0, T, TT):
            spread(z1, a, dot_nt(lt, tok[a, t0:t0 + TT, :]), t0)
    send_pair(z1, a1, s1, 0, 0)
    ins[1].wait()
    gathered(1)
    for f in range(8):
        for t0 in range(0, T, TT):
            spread(z3, f, dot_nt(r2g[f], cot[f, t0:t0 + TT, :]), t0)
    send_pair(z3, a3, s3, 1, 0)
    forward_shard(2)
    forward_shard(3)

    def rest(q, _):
        send_pair(z1, a1, s1, 0, q)
        send_pair(z3, a3, s3, 1, q)
        return 0

    lax.fori_loop(1, QS, rest, 0)
    gathered(2)
    gathered(3)

    def sum_x(k, src, dst, n, lead, sem):
        for i in range(1, NX):
            to = lax.rem(x + i, NX)
            remote(src.at[lead, pl.ds(pl.multiple_of(to * 2 * n, 2 * n), 2 * n), :], dst.at[i - 1, lead],
                   rx_s.at[sem], rx_r.at[sem], xpeer(i)).start()

    scale = 1.0 / jnp.sqrt(F32(8192.0))

    def sum_y(src, dst, ybuf, yrecv, res, n, lead, sem):
        for i in range(NX - 1):
            pass
        await_bytes(dst.at[:, lead], rx_r.at[sem])
        for half in range(2):
            total = src[lead, pl.ds(pl.multiple_of(x * 2 * n + half * n, n), n), :].astype(F32)
            for i in range(NX - 1):
                total += dst[i, lead, half * n:(half + 1) * n, :].astype(F32)

            @pl.when(yh == half)
            def _():
                res[lead] = total

            @pl.when(yh != half)
            def _():
                ybuf[lead] = total.astype(BF)

        remote(ybuf.at[lead], yrecv.at[lead], ry_s.at[sem], ry_r.at[sem], partner).start()

    def finish(yrecv, res, lead, sem):
        await_bytes(yrecv.at[lead], ry_r.at[sem])
        res[lead] = (res[lead] + yrecv[lead].astype(F32)) * scale

    def pair(q, _):
        arrived(s1, 0, q)
        arrived(s3, 1, q)
        for t0 in range(0, T, TT):
            for src, dst in ((s1, xc), (s3, fc)):
                slab = src[q, :, t0:t0 + TT].astype(F32).reshape(NF, 2, 8, TT)
                for h in range(2):
                    dst[h, :, t0:t0 + TT] = slab[:, h].reshape(NB, TT).astype(BF)

        def block(h, _):
            c = q * 2 + h
            rt[...] = rg[c].astype(F32).T.astype(BF)
            lot[...] = log_[c].astype(F32).T.astype(BF)

            def tile(j, _):
                cols = pl.ds(pl.multiple_of(j * TT, TT), TT)
                active, slope = gelu_parts(dot(rt[...], xc[h, :, cols]))
                active = active.astype(BF)
                act[:, cols] = active
                back = (dot(log_[c], fc[h, :, cols]) * slope).astype(BF)
                bp[:, cols] = back
                zf[h, :, cols] = dot(lot[...], active)
                zb[h, :, cols] = dot(rg[c], back)
                return 0

            lax.fori_loop(0, T // TT, tile, 0)
            glo_s[c] = dot_nt(act[...], fc[h]).astype(BF)
            gr_s[c] = dot_nt(xc[h], bp[...]).astype(BF)
            return 0

        lax.fori_loop(0, 2, block, 0)

        for z, abuf, sbuf, kind in ((zf, a2, s2, 2), (zb, a4, s4, 3)):
            def pack(p, _):
                rows = pl.ds(pl.multiple_of(p * 8, 8), 8)
                both = jnp.concatenate([z[0, rows, :], z[1, rows, :]], axis=0)
                abuf[q, pl.ds(pl.multiple_of(p * 16, 16), 16), :] = both.astype(BF)
                return 0

            lax.fori_loop(0, NF, pack, 0)
            ship(abuf, sbuf, kind, q)

        lead = pl.ds(q * 2, 2)
        sum_x(0, gr_s, gr_r, 16, lead, q)
        sum_x(1, glo_s, glo_r, 64, lead, QS + q)

        @pl.when(q > 0)
        def _():
            before = pl.ds(q * 2 - 2, 2)
            sum_y(gr_s, gr_r, gr_y, gr_yr, gr_o, 16, before, q - 1)
            sum_y(glo_s, glo_r, glo_y, glo_yr, glo_o, 64, before, QS + q - 1)

        return 0

    lax.fori_loop(0, QS, pair, 0)

    def gather_rows(sbuf, kind, z):
        def one_q(q, _):
            arrived(sbuf, kind, q)

            def one_k(k, _):
                rows = pl.ds(pl.multiple_of(k * 16, 16), 16)
                for tt in range(T // 128):
                    slab = sbuf[q, rows, tt * 128:(tt + 1) * 128].astype(F32)
                    for h in range(2):
                        z[tt, pl.ds(k * 8 + q * 2 + h, 8, stride=NB), :] = slab[h * 8:(h + 1) * 8]
                return 0

            lax.fori_loop(0, NF, one_k, 0)
            return 0

        lax.fori_loop(0, QS, one_q, 0)

    eye = (lax.broadcasted_iota(jnp.int32, (TT, TT), 0) == lax.broadcasted_iota(jnp.int32, (TT, TT), 1)).astype(BF)

    def block_rows(z, f):
        rows = pl.ds(pl.multiple_of(f * NB, NB), NB)
        return [z[tt, rows, :].astype(BF) for tt in range(T // 128)]

    gather_rows(s2, 2, z1)

    def last_pair():
        lead = pl.ds(QS * 2 - 2, 2)
        sum_y(gr_s, gr_r, gr_y, gr_yr, gr_o, 16, lead, QS - 1)
        sum_y(glo_s, glo_r, glo_y, glo_yr, glo_o, 64, lead, 2 * QS - 1)

    def f_block(f, _):
        y = jnp.concatenate(block_rows(z1, f), axis=1)
        gr2_s[f] = dot(y, cot[f]).astype(BF)
        for t0 in range(0, T, TT):
            yt = dot_nt(eye, y[:, t0:t0 + TT]).astype(BF)
            stage_o[f, t0:t0 + TT, :] = dot(yt, r2g[f]).astype(BF)
        pltpu.make_async_copy(stage_o.at[f], out_h.at[f], out_sem.at[0]).start()
        return 0

    lax.fori_loop(0, 8, f_block, 0)
    every = pl.ds(0, 8)
    sum_x(3, gr2_s, gr2_r, 16, every, 2 * QS)
    last_pair()

    gather_rows(s4, 3, z3)

    def a_grad(a, _):
        m = jnp.concatenate(block_rows(z3, a), axis=1)
        gl_s[a] = dot(m, tok[a]).T.astype(BF)
        return 0

    lax.fori_loop(0, 8, a_grad, 0)
    sum_x(2, gl_s, gl_r, 16, every, 2 * QS + 1)
    sum_y(gr2_s, gr2_r, gr2_y, gr2_yr, gr2_o, 16, every, 2 * QS)

    def a_block(a, _):
        m = jnp.concatenate(block_rows(z3, a), axis=1)
        for t0 in range(0, T, TT):
            mt = dot_nt(eye, m[:, t0:t0 + TT]).astype(BF)
            stage_t[a, t0:t0 + TT, :] = dot_nt(mt, lg[a]).astype(BF)
        pltpu.make_async_copy(stage_t.at[a], tg_h.at[a], out_sem.at[1]).start()
        return 0

    lax.fori_loop(0, 8, a_block, 0)
    sum_y(gl_s, gl_r, gl_y, gl_yr, gl_o, 16, every, 2 * QS + 1)

    def fin(q, _):
        lead = pl.ds(q * 2, 2)
        finish(gr_yr, gr_o, lead, q)
        finish(glo_yr, glo_o, lead, QS + q)
        return 0

    lax.fori_loop(0, QS, fin, 0)
    finish(gr2_yr, gr2_o, every, 2 * QS)
    finish(gl_yr, gl_o, every, 2 * QS + 1)

    for k, (sh, g, n) in enumerate(facs):
        await_bytes(g.at[:, pl.ds(0, n), :], agy_s.at[k])
        await_bytes(g.at[:, pl.ds(0, 6 * n), :], agx_s.at[k])

    def drain(q, _):
        for kind, buf in enumerate((a1, a3, a2, a4)):
            await_bytes(buf.at[q, pl.ds(0, 240), :], aa_s.at[kind, q])
        lead = pl.ds(q * 2, 2)
        await_bytes(gr_r.at[:, lead], rx_s.at[q])
        await_bytes(glo_r.at[:, lead], rx_s.at[QS + q])
        await_bytes(gr_yr.at[lead], ry_s.at[q])
        await_bytes(glo_yr.at[lead], ry_s.at[QS + q])
        return 0

    lax.fori_loop(0, QS, drain, 0)
    await_bytes(gr2_r, rx_s.at[2 * QS])
    await_bytes(gl_r, rx_s.at[2 * QS + 1])
    await_bytes(gr2_yr, ry_s.at[2 * QS])
    await_bytes(gl_yr, ry_s.at[2 * QS + 1])
    await_bytes(stage_o, out_sem.at[0])
    await_bytes(stage_t, out_sem.at[1])


def on_device(tokens, cotangent, left_up, right_up, left_out, right_out):
    any_, vm = pl.BlockSpec(memory_space=pl.ANY), pl.BlockSpec(memory_space=pltpu.VMEM)
    V, D = pltpu.VMEM, pltpu.SemaphoreType.DMA
    slab = V((QS, NF * 16, T), BF)
    scratch = [
        V((8, T, NB), BF), V((8, T, NB), BF),
        V((8, NB, NB), BF), V((8, NB, EX), BF), V((8, EX, NB), BF), V((8, NB, NB), BF),
        slab, slab, slab, slab, slab, slab, slab, slab,
        V((T // 128, 1024, 128), F32), V((T // 128, 1024, 128), F32),
        V((2, NB, T), BF), V((2, NB, T), BF), V((EX, NB), BF), V((NB, EX), BF),
        V((EX, T), BF), V((EX, T), BF), V((2, NB, T), F32), V((2, NB, T), F32),
        V((8, T, NB), BF), V((8, T, NB), BF),
        V((8, NB, EX), BF), V((8, EX, NB), BF), V((8, NB, NB), BF), V((8, NB, NB), BF),
        V((3, 8, 32, EX), BF), V((3, 8, 128, NB), BF), V((3, 8, 32, NB), BF), V((3, 8, 32, NB), BF),
        V((8, 16, EX), BF), V((8, 64, NB), BF), V((8, 16, NB), BF), V((8, 16, NB), BF),
        V((8, 16, EX), BF), V((8, 64, NB), BF), V((8, 16, NB), BF), V((8, 16, NB), BF),
        D((2,)), D((4,)), D((2,)),
        D((4,)), D((4,)), D((4,)), D((4,)), D((4, QS)), D((4, QS)),
        D((2 * QS + 2,)), D((2 * QS + 2,)), D((2 * QS + 2,)), D((2 * QS + 2,)),
    ]
    S = jax.ShapeDtypeStruct
    out, tg, gl, gr, glo, gr2 = pl.pallas_call(
        layer,
        out_shape=(S((8, T, NB), BF), S((8, T, NB), BF), S((8, 16, NB), F32), S((8, 16, EX), F32),
                   S((8, 64, NB), F32), S((8, 16, NB), F32)),
        in_specs=[any_] * 6,
        out_specs=(any_, any_, vm, vm, vm, vm),
        scratch_shapes=scratch,
        compiler_params=pltpu.CompilerParams(collective_id=0, has_side_effects=True, vmem_limit_bytes=62 << 20),
        cost_estimate=pl.CostEstimate(flops=8 << 30, bytes_accessed=12 << 20, transcendentals=8 << 20),
        name="monarch_layer",
    )(tokens.transpose(1, 0, 2), cotangent.transpose(1, 0, 2), left_up, right_up, left_out, right_out)
    return out.transpose(1, 0, 2), tg.transpose(1, 0, 2), gl, gr, glo, gr2


def solution(mesh):
    wide, narrow = P("dp", "feat", None), P("feat", "dp", None)
    return jax.shard_map(
        on_device,
        mesh=mesh,
        in_specs=(wide, wide, narrow, narrow, narrow, narrow),
        out_specs=(wide, wide, narrow, narrow, narrow, narrow),
        check_vma=False,
    )
```

time: 545 us -> 159 us (0.29)
  waiting for transfers between devices: 317 us -> 0 us
  Pallas kernels: 0 us -> 143 us
  blocking collectives: 91.1 us -> 0 us
  matrix products: 64.7 us -> 0 us
  starting transfers between devices: 23 us -> 0 us
  local copies, waits for them, and re-layouts: 33.2 us -> 14.7 us
  between operations: 14.2 us -> 0.67 us
    reduce_scatter x4 -> x0, waiting for transfers between devices: 239 us -> none  [the longest x1 79.1 us: on_device(): lax.psum_scatter(grad_l2, 'dp', scatter_dimension=1, tiled=True)]
    pallas_call x0 -> x1, Pallas kernels: none -> 143 us  [on_device(): pl.pallas_call(layer, out_shape=(S((8, T, NB), BF), S((8, T, NB), BF), S(...]
    all_gather x2 -> x0, blocking collectives: 91.1 us -> none  [the longest x1 56.3 us: on_device(): lax.all_gather(right_out, 'dp', axis=1, tiled=True)]
    dot_general x12 -> x0, matrix products: 64.7 us -> none  [factor_product(): return jnp.einsum(form, first, second, preferred_element_type=jnp.float32)]
    all_to_all x4 -> x0, waiting for transfers between devices: 44.6 us -> none  [the longest x1 26.6 us: on_device(): lax.all_to_all(folded, 'feat', split_axis=2, concat_axis=1, tiled=True)]
    all_gather x2 -> x0, waiting for transfers between devices: 32.9 us -> none  [the longest x1 32.9 us: on_device(): lax.all_gather(left_out, 'dp', axis=1, tiled=True)]
    all_to_all x4 -> x0, starting transfers between devices: 22.1 us -> none  [the longest x1 6.75 us: on_device(): lax.all_to_all(back_folded, 'feat', split_axis=1, concat_axis=2, tiled=True)]
    convert_element_type x4 -> x0, local copies, waits for them, and re-layouts: 13.3 us -> none  [the longest x1 4.18 us: on_device(): spread_gradient = factor_product('qyp,ydp->qdy', preactivation_gradient,...]
  transfers between devices with their start and end apart: 10 -> 0, of which waited for: 7 -> 0; matrix products, arithmetic and copies ran while one was open for 13% -> 0% of each run, Pallas kernels for 0% -> 0%
where the time goes in v1:
time: 159 us
  Pallas kernels  143 us (90%)
  local copies, waits for them, and re-layouts  14.7 us (9%)
    pallas_call x1, Pallas kernels, on_device(): pl.pallas_call(layer, out_shape=(S((8, T, NB), BF), S((8, T, NB), BF), S(...  143 us
    unnamed x16, local copies, waits for them, and re-layouts  9.77 us
    transpose x1, local copies, waits for them, and re-layouts, on_device(): cotangent.transpose(1, 0, 2)  4.98 us

profile of v1, /device:TPU:96, one launch (start us, length us, event | category | flops | bytes accessed | tf_op | source)
XLA Modules:
  0.0 158.8 jit_solution(549258251121118467)
XLA Ops:
  0.6 5.0 %copy_bitcast_fusion = (bf16[8,1024,128]{2,1,0:T(8,128)(2,1)}, bf16[8,1024,128]{2,1,0:T(8,128)(2,1)}) fusion(bf16[1024,8,128]{2,1,0:T(8,128)(2,1)} %param.7, bf16[1024,8,128]{2,1,0:T(8,128)(2,1)} %param.6), kind=kLoop, calls=%fused_computation | loop fusion | bytes 8388608 | tf_op jit(solution)/shard_map/transpose | solution.py:385
  5.6 143.4 %monarch_layer.1 = (bf16[8,1024,128]{2,1,0:T(8,128)(2,1)}, bf16[8,1024,128]{2,1,0:T(8,128)(2,1)}, f32[8,16,128]{2,1,0:T(8,128)}, f32[8,16,512]{2,1,0:T(8,128)}, ...) custom-call(bf16[8,1024,128]{2,1,0:T(8,128)(2,1)} %get-tuple-element.25.tok_h, ...), custom_call_target="tpu_custom_call" | custom-call | flops 8589934592 | bytes 12582912 | tf_op jit(solution)/shard_map/monarch_layer/pallas_call | solution.py:375
  149.0 0.0 copy-start
  149.0 4.4 %copy.14 = bf16[1024,8,128]{2,1,0:T(8,128)(2,1)} copy(bf16[1024,8,128]{2,0,1:T(8,128)(2,1)} %bitcast.7) | data formatting | bytes 4194304
  153.5 0.0 copy-done
  153.5 0.0 copy-start.4
  153.5 0.0 copy-start.2
  153.5 0.0 copy-start.1
  153.5 0.0 copy-start.3
  153.5 2.7 %copy.15 = bf16[1024,8,128]{2,1,0:T(8,128)(2,1)} copy(bf16[1024,8,128]{2,0,1:T(8,128)(2,1)S(1)} %bitcast.6) | data formatting | bytes 4194304
  156.2 0.0 copy-done.4
  156.2 0.6 copy.22
  156.8 0.0 copy-done.2
  156.8 0.7 copy.23
  157.5 0.0 copy-done.1
  157.5 0.7 copy.24
  158.2 0.0 copy-done.3
  158.2 0.6 copy.25
Async XLA Ops:
  149.0 4.4 %copy-start = (bf16[8,1024,128]{2,1,0:T(8,128)(2,1)S(1)}, bf16[8,1024,128]{2,1,0:T(8,128)(2,1)}, u32[]{:S(2)}) copy-start(bf16[8,1024,128]{2,1,0:T(8,128)(2,1)} %get-tuple-element.13) | copy-start | bytes 6291460
  153.5 2.7 %copy-start.4 = (f32[8,16,128]{2,1,0:T(8,128)S(1)}, f32[8,16,128]{2,1,0:T(8,128)}, u32[]{:S(2)}) copy-start(f32[8,16,128]{2,1,0:T(8,128)} %get-tuple-element.34) | copy-start | bytes 196612
  153.5 3.3 %copy-start.2 = (f32[8,16,512]{2,1,0:T(8,128)S(1)}, f32[8,16,512]{2,1,0:T(8,128)}, u32[]{:S(2)}) copy-start(f32[8,16,512]{2,1,0:T(8,128)} %get-tuple-element.35) | copy-start | bytes 786436
  153.5 4.0 %copy-start.1 = (f32[8,64,128]{2,1,0:T(8,128)S(1)}, f32[8,64,128]{2,1,0:T(8,128)}, u32[]{:S(2)}) copy-start(f32[8,64,128]{2,1,0:T(8,128)} %get-tuple-element.36) | copy-start | bytes 786436
  153.5 4.7 %copy-start.3 = (f32[8,16,128]{2,1,0:T(8,128)S(1)}, f32[8,16,128]{2,1,0:T(8,128)}, u32[]{:S(2)}) copy-start(f32[8,16,128]{2,1,0:T(8,128)} %get-tuple-element.37) | copy-start | bytes 196612

commit v2 on v1

--- a/solution.py
+++ b/solution.py
@@ -15,6 +15,7 @@
 T = 1024
 TT = 256
 NF = 16
+ND = 8
 NX = 4
 QS = 4
 NT = (((1,), (1,)), ((), ()))
@@ -41,13 +42,13 @@
 
 
 def layer(tok_h, cot_h, l_h, r_h, lo_h, r2_h,
-          out_h, tg_h, gl_o, gr_o, glo_o, gr2_o,
+          nat_o, nat_t, gl_o, gr_o, glo_o, gr2_o,
           tok, cot, lg, rg, log_, r2g,
           a1, a3, a2, a4, s1, s3, s2, s4, z1, z3,
-          xc, fc, rt, lot, act, bp, zf, zb, stage_o, stage_t,
+          xc, fc, rt, lot, act, bp, zf, zb,
           gr_s, glo_s, gl_s, gr2_s, gr_r, glo_r, gl_r, gr2_r,
-          gr_y, glo_y, gl_y, gr2_y, gr_yr, glo_yr, gl_yr, gr2_yr,
-          in_sem, own_sem, out_sem,
+          gr_y, glo_y, gr2_y, gr_yr, glo_yr, gr2_yr, zr, zo,
+          in_sem, own_sem,
           agy_s, agy_r, agx_s, agx_r, aa_s, aa_r, rx_s, rx_r, ry_s, ry_r):
     dp = lax.axis_index("dp")
     me = lax.axis_index("feat")
@@ -60,7 +61,7 @@
     def fpeer(i):
         return lax.rem(me + i, NF)
 
-    ins = [pltpu.make_async_copy(tok_h, tok, in_sem.at[0]), pltpu.make_async_copy(cot_h, cot, in_sem.at[1])]
+    ins = [pltpu.make_async_copy(tok_h, nat_o, in_sem.at[0]), pltpu.make_async_copy(cot_h, nat_t, in_sem.at[1])]
     for c in ins:
         c.start()
     facs = [(l_h, lg, 16), (r2_h, r2g, 16), (r_h, rg, 16), (lo_h, log_, 64)]
@@ -71,15 +72,21 @@
 
     barrier = pltpu.get_barrier_semaphore()
 
+    def dpeer(i):
+        return (lax.rem(dp + i, ND), me)
+
     def greet(i, _):
         pl.semaphore_signal(barrier, inc=1, device_id=(dp, fpeer(i)), device_id_type=MESH)
         return 0
 
     lax.fori_loop(1, NF, greet, 0)
-    for i in range(1, NX):
-        pl.semaphore_signal(barrier, inc=1, device_id=xpeer(i), device_id_type=MESH)
-    pl.semaphore_signal(barrier, inc=1, device_id=partner, device_id_type=MESH)
-    pl.semaphore_wait(barrier, NF - 1 + NX - 1 + 1)
+
+    def greet_group(i, _):
+        pl.semaphore_signal(barrier, inc=1, device_id=dpeer(i), device_id_type=MESH)
+        return 0
+
+    lax.fori_loop(1, ND, greet_group, 0)
+    pl.semaphore_wait(barrier, NF - 1 + ND - 1)
 
     def remote(src, dst, ss, rs, dev):
         return pltpu.make_async_remote_copy(src_ref=src, dst_ref=dst, send_sem=ss, recv_sem=rs,
@@ -88,9 +95,14 @@
     def await_bytes(ref, sem):
         pltpu.make_async_copy(ref, ref, sem).wait()
 
-    for k, (sh, g, n) in enumerate(facs):
+    def share_y(k):
+        sh, g, n = facs[k]
         mine = g.at[:, pl.ds(pl.multiple_of(dp * n, n), n), :]
         remote(sh, mine, agy_s.at[k], agy_r.at[k], partner).start()
+
+    def share_x(k):
+        sh, g, n = facs[k]
+        mine = g.at[:, pl.ds(pl.multiple_of(dp * n, n), n), :]
         for i in range(1, NX):
             remote(sh, mine, agx_s.at[k], agx_r.at[k], xpeer(i)).start()
 
@@ -104,10 +116,37 @@
     def gathered(k):
         sh, g, n = facs[k]
         own[k].wait()
-        await_bytes(g.at[:, pl.ds(0, 6 * n), :], agx_r.at[k])
-
-    forward_shard(0)
-    forward_shard(1)
+        await_bytes(g.at[:, pl.ds(0, (7 if k < 2 else 6) * n), :], agx_r.at[k])
+
+    def share_all(k):
+        sh, g, n = facs[k]
+        mine = g.at[:, pl.ds(pl.multiple_of(dp * n, n), n), :]
+
+        def go(i, _):
+            remote(sh, mine, agx_s.at[k], agx_r.at[k], dpeer(i)).start()
+            return 0
+
+        lax.fori_loop(1, ND, go, 0)
+
+    share_all(0)
+    share_all(1)
+    share_y(2)
+    share_y(3)
+
+    def relay(nat, dst):
+        def one(j, _):
+            rows = pl.ds(pl.multiple_of(j * 128, 128), 128)
+            zr[...] = nat[rows].astype(F32).reshape(1024, 128)
+            for a in range(8):
+                dst[a, rows, :] = zr[pl.ds(a, 128, stride=8), :].astype(BF)
+            return 0
+
+        lax.fori_loop(0, T // 128, one, 0)
+
+    ins[0].wait()
+    share_x(2)
+    share_x(3)
+    relay(nat_o, tok)
 
     def spread(z, a, res, t0):
         for h in range(TT // 128):
@@ -140,7 +179,6 @@
     def arrived(sbuf, kind, q):
         await_bytes(sbuf.at[q, pl.ds(0, 240), :], aa_r.at[kind, q])
 
-    ins[0].wait()
     gathered(0)
     for a in range(8):
         lt = lg[a].astype(F32).T.astype(BF)
@@ -148,6 +186,7 @@
             spread(z1, a, dot_nt(lt, tok[a, t0:t0 + TT, :]), t0)
     send_pair(z1, a1, s1, 0, 0)
     ins[1].wait()
+    relay(nat_t, cot)
     gathered(1)
     for f in range(8):
         for t0 in range(0, T, TT):
@@ -165,7 +204,7 @@
     gathered(2)
     gathered(3)
 
-    def sum_x(k, src, dst, n, lead, sem):
+    def sum_x(src, dst, n, lead, sem):
         for i in range(1, NX):
             to = lax.rem(x + i, NX)
             remote(src.at[lead, pl.ds(pl.multiple_of(to * 2 * n, 2 * n), 2 * n), :], dst.at[i - 1, lead],
@@ -174,8 +213,6 @@
     scale = 1.0 / jnp.sqrt(F32(8192.0))
 
     def sum_y(src, dst, ybuf, yrecv, res, n, lead, sem):
-        for i in range(NX - 1):
-            pass
         await_bytes(dst.at[:, lead], rx_r.at[sem])
         for half in range(2):
             total = src[lead, pl.ds(pl.multiple_of(x * 2 * n + half * n, n), n), :].astype(F32)
@@ -236,11 +273,12 @@
                 return 0
 
             lax.fori_loop(0, NF, pack, 0)
-            ship(abuf, sbuf, kind, q)
+            if kind == 2:
+                ship(abuf, sbuf, kind, q)
 
         lead = pl.ds(q * 2, 2)
-        sum_x(0, gr_s, gr_r, 16, lead, q)
-        sum_x(1, glo_s, glo_r, 64, lead, QS + q)
+        sum_x(gr_s, gr_r, 16, lead, q)
+        sum_x(glo_s, glo_r, 64, lead, QS + q)
 
         @pl.when(q > 0)
         def _():
@@ -252,7 +290,13 @@
 
     lax.fori_loop(0, QS, pair, 0)
 
-    def gather_rows(sbuf, kind, z):
+    def ship_back(q, _):
+        ship(a4, s4, 3, q)
+        return 0
+
+    lax.fori_loop(0, QS, ship_back, 0)
+
+    def gather_rows(sbuf, kind, z, first, last):
         def one_q(q, _):
             arrived(sbuf, kind, q)
 
@@ -267,7 +311,7 @@
             lax.fori_loop(0, NF, one_k, 0)
             return 0
 
-        lax.fori_loop(0, QS, one_q, 0)
+        lax.fori_loop(first, last, one_q, 0)
 
     eye = (lax.broadcasted_iota(jnp.int32, (TT, TT), 0) == lax.broadcasted_iota(jnp.int32, (TT, TT), 1)).astype(BF)
 
@@ -275,7 +319,7 @@
         rows = pl.ds(pl.multiple_of(f * NB, NB), NB)
         return [z[tt, rows, :].astype(BF) for tt in range(T // 128)]
 
-    gather_rows(s2, 2, z1)
+    gather_rows(s2, 2, z1, 0, QS)
 
     def last_pair():
         lead = pl.ds(QS * 2 - 2, 2)
@@ -285,18 +329,29 @@
     def f_block(f, _):
         y = jnp.concatenate(block_rows(z1, f), axis=1)
         gr2_s[f] = dot(y, cot[f]).astype(BF)
-        for t0 in range(0, T, TT):
-            yt = dot_nt(eye, y[:, t0:t0 + TT]).astype(BF)
-            stage_o[f, t0:t0 + TT, :] = dot(yt, r2g[f]).astype(BF)
-        pltpu.make_async_copy(stage_o.at[f], out_h.at[f], out_sem.at[0]).start()
         return 0
 
     lax.fori_loop(0, 8, f_block, 0)
     every = pl.ds(0, 8)
-    sum_x(3, gr2_s, gr2_r, 16, every, 2 * QS)
+    sum_x(gr2_s, gr2_r, 16, every, 2 * QS)
+
+    def write_out(z, tile_of, nat):
+        def one(j, _):
+            for f in range(8):
+                pair_of = [z[j * 2 + h, f * NB:(f + 1) * NB, :].astype(BF) for h in range(TT // 128)]
+                yt = dot_nt(eye, jnp.concatenate(pair_of, axis=1)).astype(BF)
+                zo[pl.ds(f, TT, stride=8), :] = tile_of(yt, f)
+            rows = pl.ds(pl.multiple_of(j * TT, TT), TT)
+            nat[rows] = zo[...].reshape(TT, 8, NB).astype(BF)
+            return 0
+
+        lax.fori_loop(0, T // TT, one, 0)
+
+    write_out(z1, lambda yt, f: dot(yt, r2g[f]), nat_o)
+    gather_rows(s4, 3, z3, 0, QS - 1)
     last_pair()
-
-    gather_rows(s4, 3, z3)
+    sum_y(gr2_s, gr2_r, gr2_y, gr2_yr, gr2_o, 16, every, 2 * QS)
+    gather_rows(s4, 3, z3, QS - 1, QS)
 
     def a_grad(a, _):
         m = jnp.concatenate(block_rows(z3, a), axis=1)
@@ -304,19 +359,15 @@
         return 0
 
     lax.fori_loop(0, 8, a_grad, 0)
-    sum_x(2, gl_s, gl_r, 16, every, 2 * QS + 1)
-    sum_y(gr2_s, gr2_r, gr2_y, gr2_yr, gr2_o, 16, every, 2 * QS)
-
-    def a_block(a, _):
-        m = jnp.concatenate(block_rows(z3, a), axis=1)
-        for t0 in range(0, T, TT):
-            mt = dot_nt(eye, m[:, t0:t0 + TT]).astype(BF)
-            stage_t[a, t0:t0 + TT, :] = dot_nt(mt, lg[a]).astype(BF)
-        pltpu.make_async_copy(stage_t.at[a], tg_h.at[a], out_sem.at[1]).start()
-        return 0
-
-    lax.fori_loop(0, 8, a_block, 0)
-    sum_y(gl_s, gl_r, gl_y, gl_yr, gl_o, 16, every, 2 * QS + 1)
+
+    def give(i, _):
+        to, g = dpeer(i)
+        remote(gl_s.at[:, pl.ds(pl.multiple_of(to * 16, 16), 16), :], gl_r.at[i - 1],
+               rx_s.at[2 * QS + 1], rx_r.at[2 * QS + 1], (to, g)).start()
+        return 0
+
+    lax.fori_loop(1, ND, give, 0)
+    write_out(z3, lambda yt, a: dot_nt(yt, lg[a]), nat_t)
 
     def fin(q, _):
         lead = pl.ds(q * 2, 2)
@@ -326,11 +377,16 @@
 
     lax.fori_loop(0, QS, fin, 0)
     finish(gr2_yr, gr2_o, every, 2 * QS)
-    finish(gl_yr, gl_o, every, 2 * QS + 1)
+    await_bytes(gl_r, rx_r.at[2 * QS + 1])
+    total = gl_s[:, pl.ds(pl.multiple_of(dp * 16, 16), 16), :].astype(F32)
+    for i in range(ND - 1):
+        total += gl_r[i].astype(F32)
+    gl_o[...] = total * scale
 
     for k, (sh, g, n) in enumerate(facs):
-        await_bytes(g.at[:, pl.ds(0, n), :], agy_s.at[k])
-        await_bytes(g.at[:, pl.ds(0, 6 * n), :], agx_s.at[k])
+        if k >= 2:
+            await_bytes(g.at[:, pl.ds(0, n), :], agy_s.at[k])
+        await_bytes(g.at[:, pl.ds(0, (7 if k < 2 else 6) * n), :], agx_s.at[k])
 
     def drain(q, _):
         for kind, buf in enumerate((a1, a3, a2, a4)):
@@ -346,9 +402,14 @@
     await_bytes(gr2_r, rx_s.at[2 * QS])
     await_bytes(gl_r, rx_s.at[2 * QS + 1])
     await_bytes(gr2_yr, ry_s.at[2 * QS])
-    await_bytes(gl_yr, ry_s.at[2 * QS + 1])
-    await_bytes(stage_o, out_sem.at[0])
-    await_bytes(stage_t, out_sem.at[1])
+
+
+def copy_all(*refs):
+    copies = [pltpu.make_async_copy(refs[i], refs[6 + i], refs[12].at[i]) for i in range(6)]
+    for c in copies:
+        c.start()
+    for c in copies:
+        c.wait()
 
 
 def on_device(tokens, cotangent, left_up, right_up, left_out, right_out):
@@ -362,28 +423,36 @@
         V((T // 128, 1024, 128), F32), V((T // 128, 1024, 128), F32),
         V((2, NB, T), BF), V((2, NB, T), BF), V((EX, NB), BF), V((NB, EX), BF),
         V((EX, T), BF), V((EX, T), BF), V((2, NB, T), F32), V((2, NB, T), F32),
-        V((8, T, NB), BF), V((8, T, NB), BF),
         V((8, NB, EX), BF), V((8, EX, NB), BF), V((8, NB, NB), BF), V((8, NB, NB), BF),
-        V((3, 8, 32, EX), BF), V((3, 8, 128, NB), BF), V((3, 8, 32, NB), BF), V((3, 8, 32, NB), BF),
-        V((8, 16, EX), BF), V((8, 64, NB), BF), V((8, 16, NB), BF), V((8, 16, NB), BF),
-        V((8, 16, EX), BF), V((8, 64, NB), BF), V((8, 16, NB), BF), V((8, 16, NB), BF),
-        D((2,)), D((4,)), D((2,)),
+        V((3, 8, 32, EX), BF), V((3, 8, 128, NB), BF), V((7, 8, 16, NB), BF), V((3, 8, 32, NB), BF),
+        V((8, 16, EX), BF), V((8, 64, NB), BF), V((8, 16, NB), BF),
+        V((8, 16, EX), BF), V((8, 64, NB), BF), V((8, 16, NB), BF),
+        V((1024, 128), F32), V((TT * 8, NB), F32),
+        D((2,)), D((4,)),
         D((4,)), D((4,)), D((4,)), D((4,)), D((4, QS)), D((4, QS)),
-        D((2 * QS + 2,)), D((2 * QS + 2,)), D((2 * QS + 2,)), D((2 * QS + 2,)),
+        D((2 * QS + 2,)), D((2 * QS + 2,)), D((2 * QS + 1,)), D((2 * QS + 1,)),
     ]
     S = jax.ShapeDtypeStruct
-    out, tg, gl, gr, glo, gr2 = pl.pallas_call(
+    results = pl.pallas_call(
         layer,
-        out_shape=(S((8, T, NB), BF), S((8, T, NB), BF), S((8, 16, NB), F32), S((8, 16, EX), F32),
-                   S((8, 64, NB), F32), S((8, 16, NB), F32)),
+        out_shape=(V((T, 8, NB), BF), V((T, 8, NB), BF), V((8, 16, NB), F32), V((8, 16, EX), F32),
+                   V((8, 64, NB), F32), V((8, 16, NB), F32)),
         in_specs=[any_] * 6,
-        out_specs=(any_, any_, vm, vm, vm, vm),
+        out_specs=(vm,) * 6,
         scratch_shapes=scratch,
-        compiler_params=pltpu.CompilerParams(collective_id=0, has_side_effects=True, vmem_limit_bytes=62 << 20),
+        compiler_params=pltpu.CompilerParams(collective_id=0, has_side_effects=True, vmem_limit_bytes=52 << 20),
         cost_estimate=pl.CostEstimate(flops=8 << 30, bytes_accessed=12 << 20, transcendentals=8 << 20),
         name="monarch_layer",
-    )(tokens.transpose(1, 0, 2), cotangent.transpose(1, 0, 2), left_up, right_up, left_out, right_out)
-    return out.transpose(1, 0, 2), tg.transpose(1, 0, 2), gl, gr, glo, gr2
+    )(tokens, cotangent, left_up, right_up, left_out, right_out)
+    return pl.pallas_call(
+        copy_all,
+        out_shape=tuple(S(r.shape, r.dtype) for r in results),
+        in_specs=[vm] * 6,
+        out_specs=(any_,) * 6,
+        scratch_shapes=[D((6,))],
+        compiler_params=pltpu.CompilerParams(vmem_limit_bytes=1 << 20),
+        name="copy_results",
+    )(*[pltpu.with_memory_space_constraint(r, V) for r in results])
 
 
 def solution(mesh):

time: 159 us -> 130 us (0.82)
  local copies, waits for them, and re-layouts: 14.7 us -> 0 us
  Pallas kernels: 143 us -> 129 us
    pallas_call x1 -> x2, Pallas kernels: 143 us -> 129 us  [the longest x1 127 us: on_device(): pl.pallas_call(layer, out_shape=(V((T, 8, NB), BF), V((T, 8, NB), BF), V(...]
    unnamed x16 -> x0, local copies, waits for them, and re-layouts: 9.77 us -> none
    transpose x1 -> x0, local copies, waits for them, and re-layouts: 4.98 us -> none  [on_device(): cotangent.transpose(1, 0, 2)]
where the time goes in v2:
time: 130 us
  Pallas kernels  129 us (99%)
    pallas_call x1, Pallas kernels, on_device(): pl.pallas_call(layer, out_shape=(V((T, 8, NB), BF), V((T, 8, NB), BF), V(...  127 us

profile of v2, /device:TPU:96, one launch (start us, length us, event | category | flops | bytes accessed | tf_op | source)
XLA Modules:
  0.0 130.0 jit_solution(14441814459370527080)
XLA Ops:
  0.6 127.2 %monarch_layer.1 = (bf16[1024,8,128]{2,1,0:T(8,128)(2,1)S(1)}, bf16[1024,8,128]{2,1,0:T(8,128)(2,1)S(1)}, f32[8,16,128]{2,1,0:T(8,128)S(1)}, f32[8,16,512]{2,1,0...) custom-call(bf16[1024,8,128]{2,1,0:T(8,128)(2,1)} %tok_h.1, bf16[1024,8,128]{2,1,0:T(8,128)(2,1)} %cot_h.1, ...), custom_call_target="tpu_custom_call" | custom-call | flops 8589934592 | bytes 12582912 | tf_op jit(solution)/shard_map/monarch_layer/pallas_call | solution.py:436
  127.8 2.2 %copy_results.1 = (bf16[1024,8,128]{2,1,0:T(8,128)(2,1)}, bf16[1024,8,128]{2,1,0:T(8,128)(2,1)}, f32[8,16,128]{2,1,0:T(8,128)}, f32[8,16,512]{2,1,0:T(8,128)}, f...) custom-call(bf16[1024,8,128]{2,1,0:T(8,128)(2,1)S(1)} %get-tuple-element.12.refs_0_, ...), custom_call_target="tpu_custom_call" | custom-call | tf_op jit(solution)/shard_map/copy_results/pallas_call | solution.py:447

commit v3 on v2

--- a/solution.py
+++ b/solution.py
@@ -47,7 +47,7 @@
           a1, a3, a2, a4, s1, s3, s2, s4, z1, z3,
           xc, fc, rt, lot, act, bp, zf, zb,
           gr_s, glo_s, gl_s, gr2_s, gr_r, glo_r, gl_r, gr2_r,
-          gr_y, glo_y, gr2_y, gr_yr, glo_yr, gr2_yr, zr, zo,
+          gr_y, glo_y, gr2_y, gr_yr, glo_yr, gr2_yr, zr, zo, gl_acc,
           in_sem, own_sem,
           agy_s, agy_r, agx_s, agx_r, aa_s, aa_r, rx_s, rx_r, ry_s, ry_r):
     dp = lax.axis_index("dp")
@@ -98,13 +98,14 @@
     def share_y(k):
         sh, g, n = facs[k]
         mine = g.at[:, pl.ds(pl.multiple_of(dp * n, n), n), :]
-        remote(sh, mine, agy_s.at[k], agy_r.at[k], partner).start()
+        own[k].wait()
+        remote(mine, mine, agy_s.at[k], agy_r.at[k], partner).start()
 
     def share_x(k):
         sh, g, n = facs[k]
         mine = g.at[:, pl.ds(pl.multiple_of(dp * n, n), n), :]
         for i in range(1, NX):
-            remote(sh, mine, agx_s.at[k], agx_r.at[k], xpeer(i)).start()
+            remote(mine, mine, agx_s.at[k], agx_r.at[k], xpeer(i)).start()
 
     def forward_shard(k):
         sh, g, n = facs[k]
@@ -115,23 +116,10 @@
 
     def gathered(k):
         sh, g, n = facs[k]
-        own[k].wait()
-        await_bytes(g.at[:, pl.ds(0, (7 if k < 2 else 6) * n), :], agx_r.at[k])
-
-    def share_all(k):
-        sh, g, n = facs[k]
-        mine = g.at[:, pl.ds(pl.multiple_of(dp * n, n), n), :]
-
-        def go(i, _):
-            remote(sh, mine, agx_s.at[k], agx_r.at[k], dpeer(i)).start()
-            return 0
-
-        lax.fori_loop(1, ND, go, 0)
-
-    share_all(0)
-    share_all(1)
-    share_y(2)
-    share_y(3)
+        await_bytes(g.at[:, pl.ds(0, 6 * n), :], agx_r.at[k])
+
+    share_y(0)
+    share_x(0)
 
     def relay(nat, dst):
         def one(j, _):
@@ -143,10 +131,13 @@
 
         lax.fori_loop(0, T // 128, one, 0)
 
+    forward_shard(0)
+    for k in range(1, 4):
+        share_y(k)
+    share_x(1)
     ins[0].wait()
-    share_x(2)
-    share_x(3)
     relay(nat_o, tok)
+    forward_shard(1)
 
     def spread(z, a, res, t0):
         for h in range(TT // 128):
@@ -185,6 +176,9 @@
         for t0 in range(0, T, TT):
             spread(z1, a, dot_nt(lt, tok[a, t0:t0 + TT, :]), t0)
     send_pair(z1, a1, s1, 0, 0)
+    share_x(2)
+    share_x(3)
+    send_pair(z1, a1, s1, 0, 1)
     ins[1].wait()
     relay(nat_t, cot)
     gathered(1)
@@ -194,13 +188,14 @@
     send_pair(z3, a3, s3, 1, 0)
     forward_shard(2)
     forward_shard(3)
+    send_pair(z3, a3, s3, 1, 1)
 
     def rest(q, _):
         send_pair(z1, a1, s1, 0, q)
         send_pair(z3, a3, s3, 1, q)
         return 0
 
-    lax.fori_loop(1, QS, rest, 0)
+    lax.fori_loop(2, QS, rest, 0)
     gathered(2)
     gathered(3)
 
@@ -212,7 +207,7 @@
 
     scale = 1.0 / jnp.sqrt(F32(8192.0))
 
-    def sum_y(src, dst, ybuf, yrecv, res, n, lead, sem):
+    def sum_y(src, dst, ybuf, res, n, lead, sem):
         await_bytes(dst.at[:, lead], rx_r.at[sem])
         for half in range(2):
             total = src[lead, pl.ds(pl.multiple_of(x * 2 * n + half * n, n), n), :].astype(F32)
@@ -227,6 +222,7 @@
             def _():
                 ybuf[lead] = total.astype(BF)
 
+    def send_y(ybuf, yrecv, lead, sem):
         remote(ybuf.at[lead], yrecv.at[lead], ry_s.at[sem], ry_r.at[sem], partner).start()
 
     def finish(yrecv, res, lead, sem):
@@ -283,27 +279,46 @@
         @pl.when(q > 0)
         def _():
             before = pl.ds(q * 2 - 2, 2)
-            sum_y(gr_s, gr_r, gr_y, gr_yr, gr_o, 16, before, q - 1)
-            sum_y(glo_s, glo_r, glo_y, glo_yr, glo_o, 64, before, QS + q - 1)
+            sum_y(gr_s, gr_r, gr_y, gr_o, 16, before, q - 1)
+            sum_y(glo_s, glo_r, glo_y, glo_o, 64, before, QS + q - 1)
 
         return 0
 
     lax.fori_loop(0, QS, pair, 0)
 
-    def ship_back(q, _):
-        ship(a4, s4, 3, q)
-        return 0
-
-    lax.fori_loop(0, QS, ship_back, 0)
-
-    def gather_rows(sbuf, kind, z, first, last):
+    def quarter(j):
+        return pl.ds(pl.multiple_of(j * TT, TT), TT)
+
+    def ship_back(j, _):
+        mine = pl.ds(pl.multiple_of(me * 16, 16), 16)
+
+        def go(i, _):
+            p = fpeer(i)
+            rows = pl.ds(pl.multiple_of(p * 16, 16), 16)
+            remote(a4.at[:, rows, quarter(j)], s4.at[:, mine, quarter(j)], aa_s.at[3, j], aa_r.at[3, j], (dp, p)).start()
+            return 0
+
+        lax.fori_loop(1, NF, go, 0)
+        s4[:, mine, quarter(j)] = a4[:, mine, quarter(j)]
+        return 0
+
+    lax.fori_loop(0, T // TT, ship_back, 0)
+
+    def send_pair_y(q, _):
+        lead = pl.ds(q * 2, 2)
+        send_y(gr_y, gr_yr, lead, q)
+        send_y(glo_y, glo_yr, lead, QS + q)
+        return 0
+
+    lax.fori_loop(0, QS - 1, send_pair_y, 0)
+
+    def gather_rows(sbuf, z, first, count):
         def one_q(q, _):
-            arrived(sbuf, kind, q)
-
             def one_k(k, _):
                 rows = pl.ds(pl.multiple_of(k * 16, 16), 16)
-                for tt in range(T // 128):
-                    slab = sbuf[q, rows, tt * 128:(tt + 1) * 128].astype(F32)
+                for i in range(count):
+                    tt = first + i
+                    slab = sbuf[q, rows, pl.ds(pl.multiple_of(tt * 128, 128), 128)].astype(F32)
                     for h in range(2):
                         z[tt, pl.ds(k * 8 + q * 2 + h, 8, stride=NB), :] = slab[h * 8:(h + 1) * 8]
                 return 0
@@ -311,54 +326,72 @@
             lax.fori_loop(0, NF, one_k, 0)
             return 0
 
-        lax.fori_loop(first, last, one_q, 0)
+        lax.fori_loop(0, QS, one_q, 0)
 
     eye = (lax.broadcasted_iota(jnp.int32, (TT, TT), 0) == lax.broadcasted_iota(jnp.int32, (TT, TT), 1)).astype(BF)
 
-    def block_rows(z, f):
+    def block_rows(z, f, first, count):
         rows = pl.ds(pl.multiple_of(f * NB, NB), NB)
-        return [z[tt, rows, :].astype(BF) for tt in range(T // 128)]
-
-    gather_rows(s2, 2, z1, 0, QS)
+        return jnp.concatenate([z[first + i, rows, :].astype(BF) for i in range(count)], axis=1)
+
+    def folded_here(q, _):
+        arrived(s2, 2, q)
+        return 0
+
+    lax.fori_loop(0, QS, folded_here, 0)
+    gather_rows(s2, z1, 0, T // 128)
 
     def last_pair():
         lead = pl.ds(QS * 2 - 2, 2)
-        sum_y(gr_s, gr_r, gr_y, gr_yr, gr_o, 16, lead, QS - 1)
-        sum_y(glo_s, glo_r, glo_y, glo_yr, glo_o, 64, lead, 2 * QS - 1)
+        sum_y(gr_s, gr_r, gr_y, gr_o, 16, lead, QS - 1)
+        sum_y(glo_s, glo_r, glo_y, glo_o, 64, lead, 2 * QS - 1)
+        send_pair_y(QS - 1, 0)
 
     def f_block(f, _):
-        y = jnp.concatenate(block_rows(z1, f), axis=1)
-        gr2_s[f] = dot(y, cot[f]).astype(BF)
+        gr2_s[f] = dot(block_rows(z1, f, 0, T // 128), cot[f]).astype(BF)
         return 0
 
     lax.fori_loop(0, 8, f_block, 0)
     every = pl.ds(0, 8)
     sum_x(gr2_s, gr2_r, 16, every, 2 * QS)
 
-    def write_out(z, tile_of, nat):
-        def one(j, _):
-            for f in range(8):
-                pair_of = [z[j * 2 + h, f * NB:(f + 1) * NB, :].astype(BF) for h in range(TT // 128)]
-                yt = dot_nt(eye, jnp.concatenate(pair_of, axis=1)).astype(BF)
-                zo[pl.ds(f, TT, stride=8), :] = tile_of(yt, f)
-            rows = pl.ds(pl.multiple_of(j * TT, TT), TT)
-            nat[rows] = zo[...].reshape(TT, 8, NB).astype(BF)
-            return 0
-
-        lax.fori_loop(0, T // TT, one, 0)
-
-    write_out(z1, lambda yt, f: dot(yt, r2g[f]), nat_o)
-    gather_rows(s4, 3, z3, 0, QS - 1)
+    def write_tile(z, tile_of, nat, j):
+        for f in range(8):
+            yt = dot_nt(eye, block_rows(z, f, j * 2, 2)).astype(BF)
+            zo[pl.ds(f, TT, stride=8), :] = tile_of(yt, f)
+        nat[quarter(j)] = zo[...].reshape(TT, 8, NB).astype(BF)
+
+    def out_tile(j, _):
+        write_tile(z1, lambda yt, f: dot(yt, r2g[f]), nat_o, j)
+        return 0
+
+    lax.fori_loop(0, T // TT, out_tile, 0)
     last_pair()
-    sum_y(gr2_s, gr2_r, gr2_y, gr2_yr, gr2_o, 16, every, 2 * QS)
-    gather_rows(s4, 3, z3, QS - 1, QS)
-
-    def a_grad(a, _):
-        m = jnp.concatenate(block_rows(z3, a), axis=1)
-        gl_s[a] = dot(m, tok[a]).T.astype(BF)
-        return 0
-
-    lax.fori_loop(0, 8, a_grad, 0)
+    sum_y(gr2_s, gr2_r, gr2_y, gr2_o, 16, every, 2 * QS)
+    send_y(gr2_y, gr2_yr, every, 2 * QS)
+
+    def back_tile(j):
+        write_tile(z3, lambda yt, a: dot_nt(yt, lg[a]), nat_t, j)
+
+    for a in range(8):
+        gl_acc[a] = jnp.zeros((NB, NB), F32)
+
+    def a_stage(j, _):
+        await_bytes(s4.at[:, pl.ds(0, 240), quarter(j)], aa_r.at[3, j])
+        gather_rows(s4, z3, j * 2, 2)
+        for a in range(8):
+            gl_acc[a] += dot(block_rows(z3, a, j * 2, 2), tok[a, quarter(j), :])
+        return 0
+
+    def a_early(j, _):
+        a_stage(j, 0)
+        back_tile(j)
+        return 0
+
+    lax.fori_loop(0, T // TT - 1, a_early, 0)
+    a_stage(T // TT - 1, 0)
+    for a in range(8):
+        gl_s[a] = gl_acc[a].T.astype(BF)
 
     def give(i, _):
         to, g = dpeer(i)
@@ -367,7 +400,7 @@
         return 0
 
     lax.fori_loop(1, ND, give, 0)
-    write_out(z3, lambda yt, a: dot_nt(yt, lg[a]), nat_t)
+    back_tile(T // TT - 1)
 
     def fin(q, _):
         lead = pl.ds(q * 2, 2)
@@ -384,13 +417,13 @@
     gl_o[...] = total * scale
 
     for k, (sh, g, n) in enumerate(facs):
-        if k >= 2:
-            await_bytes(g.at[:, pl.ds(0, n), :], agy_s.at[k])
-        await_bytes(g.at[:, pl.ds(0, (7 if k < 2 else 6) * n), :], agx_s.at[k])
+        await_bytes(g.at[:, pl.ds(0, n), :], agy_s.at[k])
+        await_bytes(g.at[:, pl.ds(0, 6 * n), :], agx_s.at[k])
 
     def drain(q, _):
-        for kind, buf in enumerate((a1, a3, a2, a4)):
+        for kind, buf in enumerate((a1, a3, a2)):
             await_bytes(buf.at[q, pl.ds(0, 240), :], aa_s.at[kind, q])
+        await_bytes(a4.at[:, pl.ds(0, 240), quarter(q)], aa_s.at[3, q])
         lead = pl.ds(q * 2, 2)
         await_bytes(gr_r.at[:, lead], rx_s.at[q])
         await_bytes(glo_r.at[:, lead], rx_s.at[QS + q])
@@ -404,8 +437,16 @@
     await_bytes(gr2_yr, ry_s.at[2 * QS])
 
 
+CUTS = (4, 4, 1, 1, 1, 1)
+
+
 def copy_all(*refs):
-    copies = [pltpu.make_async_copy(refs[i], refs[6 + i], refs[12].at[i]) for i in range(6)]
+    copies = []
+    for i, cuts in enumerate(CUTS):
+        n = refs[i].shape[0] // cuts
+        for j in range(cuts):
+            rows = pl.ds(j * n, n)
+            copies.append(pltpu.make_async_copy(refs[i].at[rows], refs[6 + i].at[rows], refs[12].at[len(copies)]))
     for c in copies:
         c.start()
     for c in copies:
@@ -427,7 +468,7 @@
         V((3, 8, 32, EX), BF), V((3, 8, 128, NB), BF), V((7, 8, 16, NB), BF), V((3, 8, 32, NB), BF),
         V((8, 16, EX), BF), V((8, 64, NB), BF), V((8, 16, NB), BF),
         V((8, 16, EX), BF), V((8, 64, NB), BF), V((8, 16, NB), BF),
-        V((1024, 128), F32), V((TT * 8, NB), F32),
+        V((1024, 128), F32), V((TT * 8, NB), F32), V((8, NB, NB), F32),
         D((2,)), D((4,)),
         D((4,)), D((4,)), D((4,)), D((4,)), D((4, QS)), D((4, QS)),
         D((2 * QS + 2,)), D((2 * QS + 2,)), D((2 * QS + 1,)), D((2 * QS + 1,)),
@@ -449,7 +490,7 @@
         out_shape=tuple(S(r.shape, r.dtype) for r in results),
         in_specs=[vm] * 6,
         out_specs=(any_,) * 6,
-        scratch_shapes=[D((6,))],
+        scratch_shapes=[D((sum(CUTS),))],
         compiler_params=pltpu.CompilerParams(vmem_limit_bytes=1 << 20),
         name="copy_results",
     )(*[pltpu.with_memory_space_constraint(r, V) for r in results])

time: 130 us -> 122 us (0.938)
  Pallas kernels: 129 us -> 121 us
    pallas_call x1, Pallas kernels: 127 us -> 119 us  [on_device(): pl.pallas_call(layer, out_shape=(V((T, 8, NB), BF), V((T, 8, NB), BF), V(...]
where the time goes in v3:
time: 122 us
  Pallas kernels  121 us (99%)
    pallas_call x1, Pallas kernels, on_device(): pl.pallas_call(layer, out_shape=(V((T, 8, NB), BF), V((T, 8, NB), BF), V(...  119 us

profile of v3, /device:TPU:96, one launch (start us, length us, event | category | flops | bytes accessed | tf_op | source)
XLA Modules:
  0.0 121.7 jit_solution(2514013566856487869)
XLA Ops:
  0.6 118.8 %monarch_layer.1 = (bf16[1024,8,128]{2,1,0:T(8,128)(2,1)S(1)}, bf16[1024,8,128]{2,1,0:T(8,128)(2,1)S(1)}, f32[8,16,128]{2,1,0:T(8,128)S(1)}, f32[8,16,512]{2,1,0...) custom-call(bf16[1024,8,128]{2,1,0:T(8,128)(2,1)} %tok_h.1, bf16[1024,8,128]{2,1,0:T(8,128)(2,1)} %cot_h.1, ...), custom_call_target="tpu_custom_call" | custom-call | flops 8589934592 | bytes 12582912 | tf_op jit(solution)/shard_map/monarch_layer/pallas_call | solution.py:477
  119.4 2.3 %copy_results.1 = (bf16[1024,8,128]{2,1,0:T(8,128)(2,1)}, bf16[1024,8,128]{2,1,0:T(8,128)(2,1)}, f32[8,16,128]{2,1,0:T(8,128)}, f32[8,16,512]{2,1,0:T(8,128)}, f...) custom-call(bf16[1024,8,128]{2,1,0:T(8,128)(2,1)S(1)} %get-tuple-element.12.refs_0_, ...), custom_call_target="tpu_custom_call" | custom-call | tf_op jit(solution)/shard_map/copy_results/pallas_call | solution.py:488

commit v4 on v3

--- a/solution.py
+++ b/solution.py
@@ -18,6 +18,8 @@
 ND = 8
 NX = 4
 QS = 4
+STEPS = ((1, 2, 0), (1, 2, 1), (1, 1, 0), (1, 3, 0), (1, 1, 1), (1, 3, 1), (1, 0, 0), (1, 0, 1),
+         (0, 2, 0), (0, 2, 1), (0, 1, 0), (0, 3, 0), (0, 1, 1), (0, 3, 1), (0, 0, 1))
 NT = (((1,), (1,)), ((), ()))
 
 
@@ -58,8 +60,11 @@
     def xpeer(i):
         return (lax.rem(x + i, NX) * 2 + yh, me)
 
-    def fpeer(i):
-        return lax.rem(me + i, NF)
+    fy, fz, fc_ = lax.div(me, 8), lax.rem(lax.div(me, 2), 4), lax.rem(me, 2)
+
+    def fpeer(step):
+        dy, dz, dc = step
+        return lax.rem(fy + dy, 2) * 8 + lax.rem(fz + dz, 4) * 2 + lax.rem(fc_ + dc, 2)
 
     ins = [pltpu.make_async_copy(tok_h, nat_o, in_sem.at[0]), pltpu.make_async_copy(cot_h, nat_t, in_sem.at[1])]
     for c in ins:
@@ -76,7 +81,7 @@
         return (lax.rem(dp + i, ND), me)
 
     def greet(i, _):
-        pl.semaphore_signal(barrier, inc=1, device_id=(dp, fpeer(i)), device_id_type=MESH)
+        pl.semaphore_signal(barrier, inc=1, device_id=(dp, lax.rem(me + i, NF)), device_id_type=MESH)
         return 0
 
     lax.fori_loop(1, NF, greet, 0)
@@ -118,8 +123,10 @@
         sh, g, n = facs[k]
         await_bytes(g.at[:, pl.ds(0, 6 * n), :], agx_r.at[k])
 
-    share_y(0)
-    share_x(0)
+    share_y(1)
+    share_x(1)
+    for k in (0, 2, 3):
+        share_y(k)
 
     def relay(nat, dst):
         def one(j, _):
@@ -131,64 +138,59 @@
 
         lax.fori_loop(0, T // 128, one, 0)
 
+    forward_shard(1)
+    share_x(0)
+    ins[1].wait()
+    relay(nat_t, cot)
     forward_shard(0)
-    for k in range(1, 4):
-        share_y(k)
-    share_x(1)
-    ins[0].wait()
-    relay(nat_o, tok)
-    forward_shard(1)
 
     def spread(z, a, res, t0):
         for h in range(TT // 128):
             z[t0 // 128 + h, pl.ds(a, NB, stride=8), :] = res[:, h * 128:(h + 1) * 128]
 
-    def send_pair(z, abuf, sbuf, kind, q):
-        def one(i, _):
-            p = fpeer(i)
+    def send_pair(z, abuf, sbuf, kind, q, first=0, end=T // 128):
+        def one(p, _):
             rows = pl.ds(pl.multiple_of(p * 16, 16), 16)
-            for tt in range(T // 128):
+            for tt in range(first, end):
                 piece = z[tt, pl.ds(pl.multiple_of(p * 64 + q * 16, 16), 16), :].astype(BF)
                 abuf[q, rows, tt * 128:(tt + 1) * 128] = piece
             return 0
 
         lax.fori_loop(0, NF, one, 0)
-        ship(abuf, sbuf, kind, q)
-
-    def ship(abuf, sbuf, kind, q):
+        ship(abuf, sbuf, kind, q, pl.ds(first * 128, (end - first) * 128))
+
+    def ship(abuf, sbuf, kind, q, cols=pl.ds(0, T)):
         mine = pl.ds(pl.multiple_of(me * 16, 16), 16)
 
-        def go(i, _):
-            p = fpeer(i)
+        for step in STEPS:
+            p = fpeer(step)
             rows = pl.ds(pl.multiple_of(p * 16, 16), 16)
-            remote(abuf.at[q, rows, :], sbuf.at[q, mine, :], aa_s.at[kind, q], aa_r.at[kind, q], (dp, p)).start()
-            return 0
-
-        lax.fori_loop(1, NF, go, 0)
-        sbuf[q, mine, :] = abuf[q, mine, :]
+            remote(abuf.at[q, rows, cols], sbuf.at[q, mine, cols], aa_s.at[kind, q], aa_r.at[kind, q], (dp, p)).start()
+        sbuf[q, mine, cols] = abuf[q, mine, cols]
 
     def arrived(sbuf, kind, q):
         await_bytes(sbuf.at[q, pl.ds(0, 240), :], aa_r.at[kind, q])
 
+    gathered(1)
+    for first in (0, 4):
+        for f in range(8):
+            for t0 in range(first * 128, first * 128 + T // 2, TT):
+                spread(z3, f, dot_nt(r2g[f], cot[f, t0:t0 + TT, :]), t0)
+        send_pair(z3, a3, s3, 1, 0, first, first + 4)
+    share_x(2)
+    share_x(3)
+    send_pair(z3, a3, s3, 1, 1)
+    ins[0].wait()
+    relay(nat_o, tok)
     gathered(0)
     for a in range(8):
         lt = lg[a].astype(F32).T.astype(BF)
         for t0 in range(0, T, TT):
             spread(z1, a, dot_nt(lt, tok[a, t0:t0 + TT, :]), t0)
     send_pair(z1, a1, s1, 0, 0)
-    share_x(2)
-    share_x(3)
-    send_pair(z1, a1, s1, 0, 1)
-    ins[1].wait()
-    relay(nat_t, cot)
-    gathered(1)
-    for f in range(8):
-        for t0 in range(0, T, TT):
-            spread(z3, f, dot_nt(r2g[f], cot[f, t0:t0 + TT, :]), t0)
-    send_pair(z3, a3, s3, 1, 0)
     forward_shard(2)
     forward_shard(3)
-    send_pair(z3, a3, s3, 1, 1)
+    send_pair(z1, a1, s1, 0, 1)
 
     def rest(q, _):
         send_pair(z1, a1, s1, 0, q)
@@ -292,13 +294,10 @@
     def ship_back(j, _):
         mine = pl.ds(pl.multiple_of(me * 16, 16), 16)
 
-        def go(i, _):
-            p = fpeer(i)
+        for step in STEPS:
+            p = fpeer(step)
             rows = pl.ds(pl.multiple_of(p * 16, 16), 16)
             remote(a4.at[:, rows, quarter(j)], s4.at[:, mine, quarter(j)], aa_s.at[3, j], aa_r.at[3, j], (dp, p)).start()
-            return 0
-
-        lax.fori_loop(1, NF, go, 0)
         s4[:, mine, quarter(j)] = a4[:, mine, quarter(j)]
         return 0
 
@@ -391,11 +390,11 @@
     lax.fori_loop(0, T // TT - 1, a_early, 0)
     a_stage(T // TT - 1, 0)
     for a in range(8):
-        gl_s[a] = gl_acc[a].T.astype(BF)
+        gl_s[:, a] = gl_acc[a].T.reshape(ND, 16, NB).astype(BF)
 
     def give(i, _):
         to, g = dpeer(i)
-        remote(gl_s.at[:, pl.ds(pl.multiple_of(to * 16, 16), 16), :], gl_r.at[i - 1],
+        remote(gl_s.at[to], gl_r.at[i - 1],
                rx_s.at[2 * QS + 1], rx_r.at[2 * QS + 1], (to, g)).start()
         return 0
 
@@ -411,7 +410,7 @@
     lax.fori_loop(0, QS, fin, 0)
     finish(gr2_yr, gr2_o, every, 2 * QS)
     await_bytes(gl_r, rx_r.at[2 * QS + 1])
-    total = gl_s[:, pl.ds(pl.multiple_of(dp * 16, 16), 16), :].astype(F32)
+    total = gl_s[dp].astype(F32)
     for i in range(ND - 1):
         total += gl_r[i].astype(F32)
     gl_o[...] = total * scale
@@ -464,7 +463,7 @@
         V((T // 128, 1024, 128), F32), V((T // 128, 1024, 128), F32),
         V((2, NB, T), BF), V((2, NB, T), BF), V((EX, NB), BF), V((NB, EX), BF),
         V((EX, T), BF), V((EX, T), BF), V((2, NB, T), F32), V((2, NB, T), F32),
-        V((8, NB, EX), BF), V((8, EX, NB), BF), V((8, NB, NB), BF), V((8, NB, NB), BF),
+        V((8, NB, EX), BF), V((8, EX, NB), BF), V((ND, 8, 16, NB), BF), V((8, NB, NB), BF),
         V((3, 8, 32, EX), BF), V((3, 8, 128, NB), BF), V((7, 8, 16, NB), BF), V((3, 8, 32, NB), BF),
         V((8, 16, EX), BF), V((8, 64, NB), BF), V((8, 16, NB), BF),
         V((8, 16, EX), BF), V((8, 64, NB), BF), V((8, 16, NB), BF),

time: 122 us -> 121 us (level); the launches traced: 122 us -> 119 us
  Pallas kernels: 121 us -> 118 us
    pallas_call x1, Pallas kernels: 119 us -> 116 us  [on_device(): pl.pallas_call(layer, out_shape=(V((T, 8, NB), BF), V((T, 8, NB), BF), V(...]
where the time goes in v4:
time: 121 us; the launch traced here: 119 us
  Pallas kernels  118 us (98%)
    pallas_call x1, Pallas kernels, on_device(): pl.pallas_call(layer, out_shape=(V((T, 8, NB), BF), V((T, 8, NB), BF), V(...  116 us

profile of v4, /device:TPU:96, one launch (start us, length us, event | category | flops | bytes accessed | tf_op | source)
XLA Modules:
  0.0 118.9 jit_solution(14112735770714107909)
XLA Ops:
  0.6 116.0 %monarch_layer.1 = (bf16[1024,8,128]{2,1,0:T(8,128)(2,1)S(1)}, bf16[1024,8,128]{2,1,0:T(8,128)(2,1)S(1)}, f32[8,16,128]{2,1,0:T(8,128)S(1)}, f32[8,16,512]{2,1,0...) custom-call(bf16[1024,8,128]{2,1,0:T(8,128)(2,1)} %tok_h.1, bf16[1024,8,128]{2,1,0:T(8,128)(2,1)} %cot_h.1, ...), custom_call_target="tpu_custom_call" | custom-call | flops 8589934592 | bytes 12582912 | tf_op jit(solution)/shard_map/monarch_layer/pallas_call | solution.py:476
  116.7 2.3 %copy_results.1 = (bf16[1024,8,128]{2,1,0:T(8,128)(2,1)}, bf16[1024,8,128]{2,1,0:T(8,128)(2,1)}, f32[8,16,128]{2,1,0:T(8,128)}, f32[8,16,512]{2,1,0:T(8,128)}, f...) custom-call(bf16[1024,8,128]{2,1,0:T(8,128)(2,1)S(1)} %get-tuple-element.12.refs_0_, ...), custom_call_target="tpu_custom_call" | custom-call | tf_op jit(solution)/shard_map/copy_results/pallas_call | solution.py:487

commit v5 on v4

--- a/solution.py
+++ b/solution.py
@@ -313,16 +313,12 @@
 
     def gather_rows(sbuf, z, first, count):
         def one_q(q, _):
-            def one_k(k, _):
-                rows = pl.ds(pl.multiple_of(k * 16, 16), 16)
+            for k in range(NF):
                 for i in range(count):
                     tt = first + i
-                    slab = sbuf[q, rows, pl.ds(pl.multiple_of(tt * 128, 128), 128)].astype(F32)
+                    slab = sbuf[q, k * 16:(k + 1) * 16, pl.ds(pl.multiple_of(tt * 128, 128), 128)].astype(F32)
                     for h in range(2):
                         z[tt, pl.ds(k * 8 + q * 2 + h, 8, stride=NB), :] = slab[h * 8:(h + 1) * 8]
-                return 0
-
-            lax.fori_loop(0, NF, one_k, 0)
             return 0
 
         lax.fori_loop(0, QS, one_q, 0)
@@ -388,17 +384,23 @@
         return 0
 
     lax.fori_loop(0, T // TT - 1, a_early, 0)
-    a_stage(T // TT - 1, 0)
-    for a in range(8):
-        gl_s[:, a] = gl_acc[a].T.reshape(ND, 16, NB).astype(BF)
-
-    def give(i, _):
-        to, g = dpeer(i)
-        remote(gl_s.at[to], gl_r.at[i - 1],
-               rx_s.at[2 * QS + 1], rx_r.at[2 * QS + 1], (to, g)).start()
-        return 0
-
-    lax.fori_loop(1, ND, give, 0)
+    last = T // TT - 1
+    await_bytes(s4.at[:, pl.ds(0, 240), quarter(last)], aa_r.at[3, last])
+    gather_rows(s4, z3, last * 2, 2)
+    for half in range(2):
+        for a in range(half * 4, half * 4 + 4):
+            term = gl_acc[a] + dot(block_rows(z3, a, last * 2, 2), tok[a, quarter(last), :])
+            gl_s[:, a] = term.T.reshape(ND, 16, NB).astype(BF)
+
+        def give(i, _):
+            to, g = dpeer(i)
+            part = pl.ds(half * 4, 4)
+            remote(gl_s.at[to, part], gl_r.at[i - 1, part],
+                   rx_s.at[2 * QS + 1], rx_r.at[2 * QS + 1], (to, g)).start()
+            return 0
+
+        lax.fori_loop(1, ND, give, 0)
+
     back_tile(T // TT - 1)
 
     def fin(q, _):

time: 121 us -> 121 us (level)
  no operation moved by 1% of the time
where the time goes in v5:
time: 121 us; the launch traced here: 119 us
  Pallas kernels  118 us (98%)
    pallas_call x1, Pallas kernels, on_device(): pl.pallas_call(layer, out_shape=(V((T, 8, NB), BF), V((T, 8, NB), BF), V(...  116 us

profile of v5, /device:TPU:96, one launch (start us, length us, event | category | flops | bytes accessed | tf_op | source)
XLA Modules:
  0.0 118.8 jit_solution(2299853583818802055)
XLA Ops:
  0.6 115.9 %monarch_layer.1 = (bf16[1024,8,128]{2,1,0:T(8,128)(2,1)S(1)}, bf16[1024,8,128]{2,1,0:T(8,128)(2,1)S(1)}, f32[8,16,128]{2,1,0:T(8,128)S(1)}, f32[8,16,512]{2,1,0...) custom-call(bf16[1024,8,128]{2,1,0:T(8,128)(2,1)} %tok_h.1, bf16[1024,8,128]{2,1,0:T(8,128)(2,1)} %cot_h.1, ...), custom_call_target="tpu_custom_call" | custom-call | flops 8589934592 | bytes 12582912 | tf_op jit(solution)/shard_map/monarch_layer/pallas_call | solution.py:478
  116.5 2.3 %copy_results.1 = (bf16[1024,8,128]{2,1,0:T(8,128)(2,1)}, bf16[1024,8,128]{2,1,0:T(8,128)(2,1)}, f32[8,16,128]{2,1,0:T(8,128)}, f32[8,16,512]{2,1,0:T(8,128)}, f...) custom-call(bf16[1024,8,128]{2,1,0:T(8,128)(2,1)S(1)} %get-tuple-element.12.refs_0_, ...), custom_call_target="tpu_custom_call" | custom-call | tf_op jit(solution)/shard_map/copy_results/pallas_call | solution.py:489
